TPU v7x, 256 devices: a whole 4x4x8 slice. The times are simulated.
256 devices in a mesh: tile: 32 (over z, x), zslab: 8 (over y, core).
Axes of the slice: x: 4, y: 4, z: 8, core: 2. Of those that a mesh axis runs over, the one named last changes fastest.
Arguments:
- band: bfloat16 [32, 4, 128, 64, 512], P('tile', None, 'zslab'), may hold values from -6 to 6
- pairs: int32 [64, 4], replicated, may hold values from 0 to 31, as said below
- extents: int32 [64, 2], replicated, may hold values from 32 to 512, as said below
Outputs:
- maps: float32 [64, 128, 32, 256], P('tile', 'zslab')
Inputs may be any that keep to these rules, and one draw needn't show every extreme that they name: `pairs`: every slot (tile, face) with tile < 32 and face < 4 is named by exactly one pair, and a pair names two different slots. `extents`: column 0 lies in 32 to 64, column 1 in 256 to 512; some pair has both at their most.
All inputs are finite; a program needn't handle non-finite values.
Results may differ from a plain program's by a relative error of at most 0.012.
The roundings to bfloat16 on the way count: a program that leaves them out, or rounds other values in their place, can miss the bound.
Values may be sent and summed in bfloat16 or wider, within the bound.
A program may use at most 64 MiB of HBM per device.

v0:
```python
import math

import jax
import jax.numpy as jnp
from jax import lax
from jax.sharding import PartitionSpec as P

GX = 32
GY = 256
GZ = 128
FACES = 4


def dft_tables(length):
    indices = jnp.arange(length, dtype=jnp.int32)
    modular = indices[:, None] * indices[None, :] % length
    angles = modular.astype(jnp.float32) * (2.0 * math.pi / length)
    factor = 1.0 / math.sqrt(length)
    return (
        (jnp.cos(angles) * factor).astype(jnp.bfloat16),
        (jnp.sin(angles) * factor).astype(jnp.bfloat16),
    )


def product(form, left, right):
    return jnp.einsum(form, left, right, preferred_element_type=jnp.float32)


def reduce_resolution(image_volume, crop_bounds):
    row_mask = (
        jnp.arange(image_volume.shape[2], dtype=jnp.int32)[None, :] < crop_bounds[:, 0:1]
    ).astype(jnp.bfloat16)
    col_mask = (
        jnp.arange(image_volume.shape[3], dtype=jnp.int32)[None, :] < crop_bounds[:, 1:2]
    ).astype(jnp.bfloat16)
    masked = image_volume * row_mask[:, None, :, None] * col_mask[:, None, None, :]
    raw_cols = jnp.arange(image_volume.shape[3], dtype=jnp.int32)
    pooled_cols = jnp.arange(GY, dtype=jnp.int32)
    pooling = jnp.where(raw_cols[:, None] // 2 == pooled_cols[None, :], 0.5, 0.0).astype(
        jnp.bfloat16
    )
    along_pooled = product("szxy,yk->szxk", masked, pooling)
    shaped = along_pooled.reshape(image_volume.shape[0], image_volume.shape[1], GX, 2, GY)
    return (shaped[:, :, :, 0, :] + shaped[:, :, :, 1, :]).astype(jnp.bfloat16)


def cross_phase(owner_re, owner_im, pairs, tiles_here):
    first_dev = pairs[:, 0] // tiles_here
    first_pos = pairs[:, 0] % tiles_here * FACES + pairs[:, 1]
    second_tile_device = pairs[:, 2] // tiles_here
    second_pos = pairs[:, 2] % tiles_here * FACES + pairs[:, 3]
    first_re = owner_re[first_dev, :, first_pos].astype(jnp.float32)
    first_im = owner_im[first_dev, :, first_pos].astype(jnp.float32)
    second_re = owner_re[second_tile_device, :, second_pos].astype(jnp.float32)
    second_im = owner_im[second_tile_device, :, second_pos].astype(jnp.float32)
    cross_re = first_re * second_re + first_im * second_im
    cross_im = first_im * second_re - first_re * second_im
    scaled = jnp.sqrt(cross_re * cross_re + cross_im * cross_im + 1.0)
    return ((cross_re / scaled).astype(jnp.bfloat16), (cross_im / scaled).astype(jnp.bfloat16))


def inverse_z(phase_real_part, phase_im, tables_z):
    w_re = (
        product("pmjk,mz->pzjk", phase_real_part, tables_z[0])
        - product("pmjk,mz->pzjk", phase_im, tables_z[1])
    ).astype(jnp.bfloat16)
    w_im = (
        product("pmjk,mz->pzjk", phase_im, tables_z[0])
        + product("pmjk,mz->pzjk", phase_real_part, tables_z[1])
    ).astype(jnp.bfloat16)
    return (w_re, w_im)


def inverse_x(w_re, w_im, tables_x):
    v_re = (
        product("pzjk,jx->pzxk", w_re, tables_x[0]) - product("pzjk,jx->pzxk", w_im, tables_x[1])
    ).astype(jnp.bfloat16)
    v_im = (
        product("pzjk,jx->pzxk", w_im, tables_x[0]) + product("pzjk,jx->pzxk", w_re, tables_x[1])
    ).astype(jnp.bfloat16)
    return (v_re, v_im)


def shards(band, pairs, extents):
    tables_x = dft_tables(GX)
    tables_y = dft_tables(GY)
    tables_z = dft_tables(GZ)
    tiles_here = band.shape[0]
    slots = tiles_here * FACES
    zrows = band.shape[2]
    tile_pos = lax.axis_index("tile")
    global_slot = tile_pos * slots + jnp.arange(slots, dtype=jnp.int32)
    first_slot = pairs[:, 0] * FACES + pairs[:, 1]
    second_slot = pairs[:, 2] * FACES + pairs[:, 3]
    matches = (
        (first_slot[None, :] == global_slot[:, None])
        | (second_slot[None, :] == global_slot[:, None])
    ).astype(jnp.int32)
    crop_bounds = jnp.sum(matches[:, :, None] * extents[None, :, :], axis=1)
    image_volume = band.reshape(slots, zrows, 2 * GX, 2 * GY)
    reduced_volume = reduce_resolution(image_volume, crop_bounds)
    y_re = product("szxy,yk->szxk", reduced_volume, tables_y[0]).astype(jnp.bfloat16)
    y_im = (-product("szxy,yk->szxk", reduced_volume, tables_y[1])).astype(jnp.bfloat16)
    x_re = (
        product("szxk,xj->szjk", y_re, tables_x[0]) + product("szxk,xj->szjk", y_im, tables_x[1])
    ).astype(jnp.bfloat16)
    x_im = (
        product("szxk,xj->szjk", y_im, tables_x[0]) - product("szxk,xj->szjk", y_re, tables_x[1])
    ).astype(jnp.bfloat16)
    kx_part = GX // lax.axis_size("zslab")
    re_in = lax.all_to_all(x_re, "zslab", split_axis=2, concat_axis=1, tiled=True)
    im_in = lax.all_to_all(x_im, "zslab", split_axis=2, concat_axis=1, tiled=True)
    out_re = (
        product("szjk,zm->msjk", re_in, tables_z[0]) + product("szjk,zm->msjk", im_in, tables_z[1])
    ).astype(jnp.bfloat16)
    out_im = (
        product("szjk,zm->msjk", im_in, tables_z[0]) - product("szjk,zm->msjk", re_in, tables_z[1])
    ).astype(jnp.bfloat16)
    tile_count = lax.axis_size("tile")
    kz_part = GZ // tile_count
    spectra = (
        lax.all_to_all(out_re, "tile", split_axis=0, concat_axis=0, tiled=True),
        lax.all_to_all(out_im, "tile", split_axis=0, concat_axis=0, tiled=True),
    )
    owner_re = spectra[0].reshape(tile_count, kz_part, slots, kx_part, GY)
    owner_im = spectra[1].reshape(tile_count, kz_part, slots, kx_part, GY)
    phase_real_part, phase_im = cross_phase(owner_re, owner_im, pairs, tiles_here)
    returned = (
        lax.all_to_all(phase_real_part, "tile", split_axis=0, concat_axis=1, tiled=True),
        lax.all_to_all(phase_im, "tile", split_axis=0, concat_axis=1, tiled=True),
    )
    w_re, w_im = inverse_z(returned[0], returned[1], tables_z)
    v_re, v_im = inverse_x(
        lax.all_to_all(w_re, "zslab", split_axis=1, concat_axis=2, tiled=True),
        lax.all_to_all(w_im, "zslab", split_axis=1, concat_axis=2, tiled=True),
        tables_x,
    )
    return product("pzxk,ky->pzxy", v_re, tables_y[0]) - product("pzxk,ky->pzxy", v_im, tables_y[1])


def solution(mesh):
    placed = (P("tile", None, "zslab", None, None), P(), P())
    return jax.shard_map(
        shards,
        mesh=mesh,
        in_specs=placed,
        out_specs=P("tile", "zslab", None, None),
        check_vma=False,
    )
```

profile of v0, /device:TPU:1, one launch (start us, length us, event | category | flops | bytes accessed | tf_op | source)
XLA Modules:
  0.0 219.9 jit_solution(18191489263805402491)
XLA Ops:
  0.0 0.8 fusion.100
  0.9 0.1 or_convert_fusion
  0.9 0.8 multiply_reduce_fusion
  1.8 0.1 fusion.85
  1.8 7.2 %reshape.185 = bf16[4,16,32,2,512]{4,3,2,1,0:T(2,128)(2,1)} reshape(bf16[1,4,16,64,512]{4,3,2,1,0:T(8,128)(2,1)} %param.3) | data formatting | bytes 8388608 | tf_op jit(solution)/shard_map/reshape | solution.py:100
  9.1 0.1 compare_convert_fusion
  9.1 3.6 %fusion.1 = f32[4,16,32,2,256]{4,2,3,1,0:T(8,128)S(1)} fusion(bf16[4,16,32,2,512]{4,3,2,1,0:T(2,128)(2,1)} %reshape.185, bf16[4,512]{1,0:T(4,128)(2,1)S(1)} %fusion.85, bf16[4,32,2]{1,2,0:T(2,128)(2,1)S(1)} %compare_convert_fusion, s32[512]{0:T(512)S(1)} %add_select_fusion.3), kind=kOutput, calls=%fused_computation.6 | convolution fusion | flops 1078329344 | bytes 8395264 | tf_op jit(solution)/shard_map/szxy,yk->szxk/dot_general | solution.py:26
  12.7 0.4 fusion.19
  13.1 1.4 negate_convert_fusion
  14.5 1.4 convolution_convert_fusion
  15.8 0.5 fusion.83
  16.3 0.5 fusion.6
  16.9 1.6 copy.118
  18.4 6.7 %all-to-all-start = ((bf16[4,16,32,256]{3,1,0,2:T(8,128)(2,1)}), bf16[4,16,32,256]{3,1,0,2:T(8,128)(2,1)S(1)}, u32[]{:S(2)}, u32[]{:S(2)}) async-start(bf16[4,16,32,256]{3,1,0,2:T(8,128)(2,1)} %copy.118), calls=%async_computation | async-start | bytes 2097152 | tf_op jit(solution)/shard_map/all_to_all | solution.py:111
  25.1 0.5 fusion.81
  25.6 0.5 fusion.7
  26.1 1.6 copy.120
  27.7 12.6 %all-to-all-done = bf16[4,16,32,256]{3,1,0,2:T(8,128)(2,1)S(1)} async-done(((bf16[4,16,32,256]{3,1,0,2:T(8,128)(2,1)}), bf16[4,16,32,256]{3,1,0,2:T(8,128)(2,1)S(1)}, u32[]{:S(2)}, u32[]{:S(2)}) %all-to-all-start) | async-done | bytes 1048608 | tf_op jit(solution)/shard_map/all_to_all | solution.py:111
  40.2 4.3 %all-to-all-start.1 = ((bf16[4,16,32,256]{3,1,0,2:T(8,128)(2,1)}), bf16[4,16,32,256]{3,1,0,2:T(8,128)(2,1)S(1)}, u32[]{:S(2)}, u32[]{:S(2)}) async-start(bf16[4,16,32,256]{3,1,0,2:T(8,128)(2,1)} %copy.120), calls=%async_computation.1 | async-start | bytes 2097152 | tf_op jit(solution)/shard_map/all_to_all | solution.py:112
  44.6 0.1 copy.119
  44.7 15.0 %all-to-all-done.1 = bf16[4,16,32,256]{3,1,0,2:T(8,128)(2,1)S(1)} async-done(((bf16[4,16,32,256]{3,1,0,2:T(8,128)(2,1)}), bf16[4,16,32,256]{3,1,0,2:T(8,128)(2,1)S(1)}, u32[]{:S(2)}, u32[]{:S(2)}) %all-to-all-start.1) | async-done | bytes 1048608 | tf_op jit(solution)/shard_map/all_to_all | solution.py:112
  59.7 1.0 copy-done
  60.7 1.3 copy.121
  62.0 0.6 fusion.61
  62.6 0.6 subtract_convert_fusion
  63.3 1.8 copy.125
  65.1 10.5 %all-to-all-start.3 = ((bf16[128,4,4,256]{3,2,1,0:T(4,128)(2,1)}), bf16[128,4,4,256]{3,2,1,0:T(4,128)(2,1)S(1)}, u32[]{:S(2)}, u32[]{:S(2)}) async-start(bf16[128,4,4,256]{3,2,1,0:T(4,128)(2,1)} %copy.125), calls=%async_computation.3 | async-start | bytes 2097152 | tf_op jit(solution)/shard_map/all_to_all | solution.py:123
  75.6 0.6 fusion.63
  76.2 0.7 add_convert_fusion
  76.9 1.8 copy.122
  78.7 22.7 %all-to-all-done.3 = bf16[128,4,4,256]{3,2,1,0:T(4,128)(2,1)S(1)} async-done(((bf16[128,4,4,256]{3,2,1,0:T(4,128)(2,1)}), bf16[128,4,4,256]{3,2,1,0:T(4,128)(2,1)S(1)}, u32[]{:S(2)}, u32[]{:S(2)}) %all-to-all-start.3) | async-done | bytes 1048608 | tf_op jit(solution)/shard_map/all_to_all | solution.py:123
  101.4 6.3 %all-to-all-start.2 = ((bf16[128,4,4,256]{3,2,1,0:T(4,128)(2,1)}), bf16[128,4,4,256]{3,2,1,0:T(4,128)(2,1)S(1)}, u32[]{:S(2)}, u32[]{:S(2)}) async-start(bf16[128,4,4,256]{3,2,1,0:T(4,128)(2,1)} %copy.122), calls=%async_computation.2 | async-start | bytes 2097152 | tf_op jit(solution)/shard_map/all_to_all | solution.py:122
  107.7 1.1 gather_fusion.3
  108.8 1.1 gather_fusion.2
  109.9 22.5 %all-to-all-done.2 = bf16[128,4,4,256]{3,2,1,0:T(4,128)(2,1)S(1)} async-done(((bf16[128,4,4,256]{3,2,1,0:T(4,128)(2,1)}), bf16[128,4,4,256]{3,2,1,0:T(4,128)(2,1)S(1)}, u32[]{:S(2)}, u32[]{:S(2)}) %all-to-all-start.2) | async-done | bytes 1048608 | tf_op jit(solution)/shard_map/all_to_all | solution.py:122
  132.4 1.1 gather_fusion.1
  133.5 1.1 gather_fusion
  134.6 1.1 divide_convert_fusion
  135.7 1.2 copy.130
  136.9 7.3 %all-to-all-start.5 = ((bf16[64,4,4,256]{3,2,1,0:T(4,128)(2,1)}), bf16[64,4,4,256]{3,2,1,0:T(4,128)(2,1)S(1)}, u32[]{:S(2)}, u32[]{:S(2)}) async-start(bf16[64,4,4,256]{3,2,1,0:T(4,128)(2,1)} %copy.130), calls=%async_computation.5 | async-start | bytes 1048576 | tf_op jit(solution)/shard_map/all_to_all | solution.py:130
  144.3 1.2 copy.128
  145.5 13.2 %all-to-all-done.5 = bf16[64,4,4,256]{3,2,1,0:T(4,128)(2,1)S(1)} async-done(((bf16[64,4,4,256]{3,2,1,0:T(4,128)(2,1)}), bf16[64,4,4,256]{3,2,1,0:T(4,128)(2,1)S(1)}, u32[]{:S(2)}, u32[]{:S(2)}) %all-to-all-start.5) | async-done | bytes 524320 | tf_op jit(solution)/shard_map/all_to_all | solution.py:130
  158.6 5.9 %all-to-all-start.4 = ((bf16[64,4,4,256]{3,2,1,0:T(4,128)(2,1)}), bf16[64,4,4,256]{3,2,1,0:T(4,128)(2,1)S(1)}, u32[]{:S(2)}, u32[]{:S(2)}) async-start(bf16[64,4,4,256]{3,2,1,0:T(4,128)(2,1)} %copy.128), calls=%async_computation.4 | async-start | bytes 1048576 | tf_op jit(solution)/shard_map/all_to_all | solution.py:129
  164.6 0.2 copy.131
  164.8 0.1 all_to_all.101
  164.9 13.5 %all-to-all-done.4 = bf16[64,4,4,256]{3,2,1,0:T(4,128)(2,1)S(1)} async-done(((bf16[64,4,4,256]{3,2,1,0:T(4,128)(2,1)}), bf16[64,4,4,256]{3,2,1,0:T(4,128)(2,1)S(1)}, u32[]{:S(2)}, u32[]{:S(2)}) %all-to-all-start.4) | async-done | bytes 524320 | tf_op jit(solution)/shard_map/all_to_all | solution.py:129
  178.4 0.2 copy.129
  178.6 0.1 all_to_all.97
  178.7 0.5 fusion.59
  179.2 0.5 fusion.16
  179.8 1.2 copy.132
  181.0 8.6 %all-to-all-start.6 = ((bf16[2,128,4,256]{3,2,0,1:T(4,128)(2,1)}), bf16[2,128,4,256]{3,2,0,1:T(4,128)(2,1)S(1)}, u32[]{:S(2)}, u32[]{:S(2)}) async-start(bf16[2,128,4,256]{3,2,0,1:T(4,128)(2,1)} %copy.132), calls=%async_computation.6 | async-start | bytes 1048576 | tf_op jit(solution)/shard_map/all_to_all | solution.py:134
  189.5 0.5 fusion.57
  190.0 0.5 fusion.15
  190.5 1.2 copy.136
  191.7 7.3 %all-to-all-done.6 = bf16[2,128,4,256]{3,2,0,1:T(4,128)(2,1)S(1)} async-done(((bf16[2,128,4,256]{3,2,0,1:T(4,128)(2,1)}), bf16[2,128,4,256]{3,2,0,1:T(4,128)(2,1)S(1)}, u32[]{:S(2)}, u32[]{:S(2)}) %all-to-all-start.6) | async-done | bytes 524320 | tf_op jit(solution)/shard_map/all_to_all | solution.py:134
  199.0 4.3 %all-to-all-start.7 = ((bf16[2,128,4,256]{3,2,0,1:T(4,128)(2,1)}), bf16[2,128,4,256]{3,2,0,1:T(4,128)(2,1)S(1)}, u32[]{:S(2)}, u32[]{:S(2)}) async-start(bf16[2,128,4,256]{3,2,0,1:T(4,128)(2,1)} %copy.136), calls=%async_computation.7 | async-start | bytes 1048576 | tf_op jit(solution)/shard_map/all_to_all | solution.py:135
  203.3 0.1 copy.133
  203.4 9.3 %all-to-all-done.7 = bf16[2,128,4,256]{3,2,0,1:T(4,128)(2,1)S(1)} async-done(((bf16[2,128,4,256]{3,2,0,1:T(4,128)(2,1)}), bf16[2,128,4,256]{3,2,0,1:T(4,128)(2,1)S(1)}, u32[]{:S(2)}, u32[]{:S(2)}) %all-to-all-start.7) | async-done | bytes 524320 | tf_op jit(solution)/shard_map/all_to_all | solution.py:135
  212.8 0.1 copy.137
  212.9 0.4 fusion.20
  213.3 1.4 fusion.26
  214.7 2.7 %fusion.14 = f32[2,16,32,256]{3,2,1,0:T(8,128)S(1)} fusion(f32[32,2,16,256]{3,0,2,1:T(8,128)} %fusion.26, bf16[2,16,32,256]{3,1,2,0:T(8,128)(2,1)S(1)} %bitcast.132), kind=kOutput, calls=%fused_computation.34 | convolution fusion | flops 152584192 | bytes 2621440 | tf_op jit(solution)/shard_map/pzxk,ky->pzxy/dot_general | solution.py:26
  217.4 2.5 %convolution_subtract_fusion = f32[2,16,32,256]{3,2,1,0:T(8,128)} fusion(f32[2,16,32,256]{3,2,1,0:T(8,128)S(1)} %fusion.14, f32[32,2,16,256]{3,0,2,1:T(8,128)S(1)} %fusion.20, bf16[2,16,32,256]{3,1,2,0:T(8,128)(2,1)S(1)} %bitcast.130), kind=kOutput, calls=%fused_computation.19 | convolution fusion | flops 152846336 | bytes 3670016 | tf_op jit(solution)/shard_map/pzxk,ky->pzxy/dot_general | solution.py:26
  (7 shorter events, 0.1 us)
Async XLA Ops:
  18.4 21.8 %all-to-all-start = ((bf16[4,16,32,256]{3,1,0,2:T(8,128)(2,1)}), bf16[4,16,32,256]{3,1,0,2:T(8,128)(2,1)S(1)}, u32[]{:S(2)}, u32[]{:S(2)}) async-start(bf16[4,16,32,256]{3,1,0,2:T(8,128)(2,1)} %copy.118), calls=%async_computation | async-start | bytes 2097152 | tf_op jit(solution)/shard_map/all_to_all | solution.py:111
  40.2 19.5 %all-to-all-start.1 = ((bf16[4,16,32,256]{3,1,0,2:T(8,128)(2,1)}), bf16[4,16,32,256]{3,1,0,2:T(8,128)(2,1)S(1)}, u32[]{:S(2)}, u32[]{:S(2)}) async-start(bf16[4,16,32,256]{3,1,0,2:T(8,128)(2,1)} %copy.120), calls=%async_computation.1 | async-start | bytes 2097152 | tf_op jit(solution)/shard_map/all_to_all | solution.py:112
  59.7 1.0 copy-start
  65.1 36.3 %all-to-all-start.3 = ((bf16[128,4,4,256]{3,2,1,0:T(4,128)(2,1)}), bf16[128,4,4,256]{3,2,1,0:T(4,128)(2,1)S(1)}, u32[]{:S(2)}, u32[]{:S(2)}) async-start(bf16[128,4,4,256]{3,2,1,0:T(4,128)(2,1)} %copy.125), calls=%async_computation.3 | async-start | bytes 2097152 | tf_op jit(solution)/shard_map/all_to_all | solution.py:123
  101.4 31.0 %all-to-all-start.2 = ((bf16[128,4,4,256]{3,2,1,0:T(4,128)(2,1)}), bf16[128,4,4,256]{3,2,1,0:T(4,128)(2,1)S(1)}, u32[]{:S(2)}, u32[]{:S(2)}) async-start(bf16[128,4,4,256]{3,2,1,0:T(4,128)(2,1)} %copy.122), calls=%async_computation.2 | async-start | bytes 2097152 | tf_op jit(solution)/shard_map/all_to_all | solution.py:122
  136.9 21.7 %all-to-all-start.5 = ((bf16[64,4,4,256]{3,2,1,0:T(4,128)(2,1)}), bf16[64,4,4,256]{3,2,1,0:T(4,128)(2,1)S(1)}, u32[]{:S(2)}, u32[]{:S(2)}) async-start(bf16[64,4,4,256]{3,2,1,0:T(4,128)(2,1)} %copy.130), calls=%async_computation.5 | async-start | bytes 1048576 | tf_op jit(solution)/shard_map/all_to_all | solution.py:130
  158.6 19.8 %all-to-all-start.4 = ((bf16[64,4,4,256]{3,2,1,0:T(4,128)(2,1)}), bf16[64,4,4,256]{3,2,1,0:T(4,128)(2,1)S(1)}, u32[]{:S(2)}, u32[]{:S(2)}) async-start(bf16[64,4,4,256]{3,2,1,0:T(4,128)(2,1)} %copy.128), calls=%async_computation.4 | async-start | bytes 1048576 | tf_op jit(solution)/shard_map/all_to_all | solution.py:129
  181.0 18.1 %all-to-all-start.6 = ((bf16[2,128,4,256]{3,2,0,1:T(4,128)(2,1)}), bf16[2,128,4,256]{3,2,0,1:T(4,128)(2,1)S(1)}, u32[]{:S(2)}, u32[]{:S(2)}) async-start(bf16[2,128,4,256]{3,2,0,1:T(4,128)(2,1)} %copy.132), calls=%async_computation.6 | async-start | bytes 1048576 | tf_op jit(solution)/shard_map/all_to_all | solution.py:134
  199.0 13.8 %all-to-all-start.7 = ((bf16[2,128,4,256]{3,2,0,1:T(4,128)(2,1)}), bf16[2,128,4,256]{3,2,0,1:T(4,128)(2,1)S(1)}, u32[]{:S(2)}, u32[]{:S(2)}) async-start(bf16[2,128,4,256]{3,2,0,1:T(4,128)(2,1)} %copy.136), calls=%async_computation.7 | async-start | bytes 1048576 | tf_op jit(solution)/shard_map/all_to_all | solution.py:135
where the time goes:
time: 221 us; the launch traced here: 220 us
  waiting for transfers between devices  116 us (52%)
  starting transfers between devices  53.9 us (24%)
  local copies, waits for them, and re-layouts  26.5 us (12%)
  matrix products  19.9 us (9%)
  other arithmetic  3.4 us (2%)
    all_to_all x1, waiting for transfers between devices, shards(): lax.all_to_all(out_im, 'tile', split_axis=0, concat_axis=0, tiled=True)  22.7 us
    all_to_all x1, waiting for transfers between devices, shards(): lax.all_to_all(out_re, 'tile', split_axis=0, concat_axis=0, tiled=True)  22.5 us
    dot_general x19, matrix products, product(): return jnp.einsum(form, left, right, preferred_element_type=jnp.float32)  19.9 us
    all_to_all x1, waiting for transfers between devices, shards(): lax.all_to_all(x_im, 'zslab', split_axis=2, concat_axis=1, tiled=True)  15 us
    all_to_all x1, waiting for transfers between devices, shards(): lax.all_to_all(phase_real_part, 'tile', split_axis=0, concat_axis=1, tile...  13.5 us
    all_to_all x1, waiting for transfers between devices, shards(): lax.all_to_all(phase_im, 'tile', split_axis=0, concat_axis=1, tiled=True)  13.2 us
    all_to_all x1, waiting for transfers between devices, shards(): lax.all_to_all(x_re, 'zslab', split_axis=2, concat_axis=1, tiled=True)  12.6 us
    all_to_all x1, starting transfers between devices, shards(): lax.all_to_all(out_im, 'tile', split_axis=0, concat_axis=0, tiled=True)  10.5 us
  transfers between devices with their start and end apart: 8, of which 8 were waited for; matrix products, arithmetic and copies ran while one was open for 5% of the time, Pallas kernels for 0%

commit v1 on v0

v1 whole, which is shorter than its diff:
```python
import functools
import math

import jax
import jax.numpy as jnp
import ml_dtypes
import numpy as np
from jax import lax
from jax.experimental import pallas as pl
from jax.experimental.pallas import tpu as pltpu
from jax.sharding import PartitionSpec as P

GX, GY, GZ, FACES = 32, 256, 128, 4
HALF = GY // 2
MESH = pl.DeviceIdType.MESH
BF = jnp.bfloat16
F32 = jnp.float32


def dft_tables(length):
    indices = np.arange(length, dtype=np.int64)
    modular = indices[:, None] * indices[None, :] % length
    angles = modular.astype(np.float32) * np.float32(2.0 * math.pi / length)
    factor = np.float32(1.0 / math.sqrt(length))
    return tuple(
        (f(angles) * factor).astype(ml_dtypes.bfloat16).astype(np.float32)
        for f in (np.cos, np.sin)
    )


def complex_forward(c, s):
    m = np.zeros((c.shape[0], 2, c.shape[1], 2), np.float32)
    m[:, 0, :, 0], m[:, 0, :, 1] = c, s
    m[:, 1, :, 1], m[:, 1, :, 0] = c, -s
    return m


def real_pair_forward(c, s):
    n = c.shape[0]
    m = np.zeros((n, 2, n, 2), np.float32)
    for part in (0, 1):
        base = part * (n // 2)
        m[base, 0, :, part], m[base, 1, :, part] = c[0], c[n // 2]
        m[base + 1 : base + n // 2, 0, :, part] = c[1 : n // 2]
        m[base + 1 : base + n // 2, 1, :, part] = -s[1 : n // 2]
    return m


def line_pair_forward(c, s):
    n = c.shape[0]
    m = real_pair_forward(c, s)
    m[0], m[n // 2] = 0.0, 0.0
    for part in (0, 1):
        m[0, part, :, part] = c[0]
        m[n // 2, part, :, part] = c[n // 2]
    return m


def complex_inverse(c, s):
    m = np.zeros((c.shape[0], 2, c.shape[1], 2), np.float32)
    m[:, 0, :, 0], m[:, 0, :, 1] = c, -s
    m[:, 1, :, 1], m[:, 1, :, 0] = c, s
    return m


def doubled(forward):
    m = np.transpose(forward, (2, 3, 0, 1)).copy()
    n = m.shape[2]
    m[:, :, 1 : n // 2] *= 2.0
    m[:, :, n // 2 + 1 :] *= 2.0
    return m


@functools.cache
def constants():
    cx, sx = dft_tables(GX)
    cy, sy = dft_tables(GY)
    cz, sz = dft_tables(GZ)
    to_y = np.concatenate([cy[:, :HALF], -sy[:, :HALF]], axis=1)
    to_y[:, HALF] = cy[:, HALF]
    pool = np.repeat(0.5 * np.eye(GY, dtype=np.float32), 2, axis=0)
    eye4, eye8 = np.eye(4, dtype=np.float32), np.eye(8, dtype=np.float32)

    split = np.zeros((2, 4, GX, 4, GX, 2), np.float32)
    for parity in (0, 1):
        split[parity, ..., parity] = np.einsum("zw,xv->zxwv", eye4, np.eye(GX, dtype=np.float32))

    def x_forward(m):
        return np.einsum("kpxq,zw->kpzqwx", m, eye4).reshape(256, 256)

    def z_forward(m):
        m = m.reshape(32, 4, 2, 8, 4, 4, 2)
        return np.transpose(m, (0, 2, 1, 3, 4, 6, 5)).reshape(256, 256)

    def z_inverse(m):
        m = m.reshape(8, 4, 4, 2, 32, 4, 2)
        return np.transpose(m, (0, 1, 3, 2, 4, 6, 5)).reshape(256, 256)

    def x_inverse(m):
        e = eye8.reshape(8, 2, 4)
        return np.einsum("xpkq,zgw->pzxkgqw", m, e).reshape(512, 512)

    from_y = np.concatenate([2.0 * cy[:HALF], -2.0 * sy[:HALF]], axis=0)
    from_y[0], from_y[HALF] = cy[0], cy[HALF]
    z_line = line_pair_forward(cz, sz)
    x_line = real_pair_forward(cx, sx)
    tables = (
        split.reshape(256, 256),
        pool,
        to_y,
        x_forward(complex_forward(cx, sx)),
        x_forward(x_line),
        z_forward(complex_forward(cz, sz)),
        z_forward(z_line),
        z_inverse(complex_inverse(cz, sz)),
        z_inverse(doubled(z_line)),
        x_inverse(complex_inverse(cx, sx)),
        x_inverse(doubled(x_line)),
        from_y,
    )
    return tuple(t.astype(ml_dtypes.bfloat16) for t in tables)


def dot(a, b):
    return jnp.dot(a, b, preferred_element_type=F32)


def body(tiles, slabs, *refs):
    (pairs_s, pairs_v, extents_v, band, *rest) = refs
    hbm_tables, rest = rest[:12], rest[12:]
    out, rest = rest[0], rest[1:]
    raw, rest = rest[0], rest[1:]
    tables, rest = rest[:12], rest[12:]
    s1, r1, s2, r2, s3, r3, s4, r4, raw_sem, table_sem, *sems = rest
    send1, recv1, send2, recv2, send3, recv3, send4, recv4 = sems
    split, pool, to_y, xf, xf0, zf, zf0, zi, zi0, xi, xi0, from_y = tables
    t = lax.axis_index("tile")
    s = lax.axis_index("zslab")

    barrier = pltpu.get_barrier_semaphore()

    @pl.loop(1, slabs)
    def _(i):
        pl.semaphore_signal(
            barrier, inc=1, device_id=(t, lax.rem(s + i, slabs)), device_id_type=MESH
        )

    @pl.loop(1, tiles)
    def _(i):
        pl.semaphore_signal(
            barrier, inc=1, device_id=(lax.rem(t + i, tiles), s), device_id_type=MESH
        )

    for f in range(FACES):
        pltpu.make_async_copy(band.at[f], raw.at[f], raw_sem.at[f]).start()
    for i in range(12):
        pltpu.make_async_copy(hbm_tables[i], tables[i], table_sem.at[i]).start()

    def table_wait(*which):
        for i in which:
            pltpu.make_async_copy(hbm_tables[i], tables[i], table_sem.at[i]).wait()

    def slab_send(src, dst, send_sem, recv_sem):
        @pl.loop(1, slabs)
        def _(i):
            d = lax.rem(s + i, slabs)
            pltpu.make_async_remote_copy(
                src_ref=src.at[d],
                dst_ref=dst.at[s],
                send_sem=send_sem,
                recv_sem=recv_sem,
                device_id=(t, d),
                device_id_type=MESH,
            ).start()

        pltpu.make_async_copy(src.at[s], dst.at[s], recv_sem).start()

    def tile_send(src, dst, send_sem, recv_sem):
        @pl.loop(1, tiles)
        def _(i):
            d = lax.rem(t + i, tiles)
            pltpu.make_async_remote_copy(
                src_ref=src.at[d],
                dst_ref=dst.at[t],
                send_sem=send_sem,
                recv_sem=recv_sem,
                device_id=(d, s),
                device_id_type=MESH,
            ).start()

        pltpu.make_async_copy(src.at[t], dst.at[t], recv_sem).start()

    def wait_for(ref, sem):
        pltpu.make_async_copy(ref, ref, sem).wait()

    lane0 = lax.broadcasted_iota(jnp.int32, (256, 128), 1) == 0
    two_lane0 = lax.broadcasted_iota(jnp.int32, (256, 256), 1) % 128 == 0
    mixed_line = (s == 0) | (s == slabs // 2)

    first = pairs_v[:, 0:1] * FACES + pairs_v[:, 1:2]
    second = pairs_v[:, 2:3] * FACES + pairs_v[:, 3:4]
    y_rows = lax.broadcasted_iota(jnp.int32, (512, 256), 0)
    x_lanes = lax.broadcasted_iota(jnp.int32, (256, 256), 1) % 64

    table_wait(0, 1, 2, 3, 4)

    def to_x(f, carry):
        slot = t * FACES + f
        named = (first == slot) | (second == slot)
        ex = jnp.sum(jnp.where(named, extents_v[:, 0:1], 0), axis=0, keepdims=True)
        ey = jnp.sum(jnp.where(named, extents_v[:, 1:2], 0), axis=0, keepdims=True)
        y_pool = jnp.where(y_rows < ey, pool[...].astype(F32), 0.0).astype(BF)
        x_split = jnp.where(x_lanes < ex, split[...].astype(F32), 0.0).astype(BF)
        pltpu.make_async_copy(band.at[f], raw.at[f], raw_sem.at[f]).wait()
        parts = []
        for half in range(2):
            y = []
            for g in range(2):
                rows = raw[f, pl.ds(512 * half + 256 * g, 256), :]
                parted = dot(x_split, rows).astype(BF)
                down = (dot(parted[:128], y_pool) + dot(parted[128:], y_pool)).astype(BF)
                y.append(dot(down, to_y[...]).astype(BF))
            stacked = jnp.concatenate(
                [
                    jnp.concatenate([y[0][:, :128], y[1][:, :128]], axis=1),
                    jnp.concatenate([y[0][:, 128:], y[1][:, 128:]], axis=1),
                ],
                axis=0,
            )
            x = jnp.where(two_lane0, dot(xf0[...], stacked), dot(xf[...], stacked))
            parts += [x[:, :128].reshape(32, 8, 128), x[:, 128:].reshape(32, 8, 128)]
        whole = jnp.concatenate(parts, axis=1).astype(BF)
        s1[f] = whole.reshape(slabs, 4, 32, 128)
        return carry

    lax.fori_loop(0, FACES, to_x, 0)

    pl.semaphore_wait(barrier, slabs - 1 + tiles - 1)
    for f in range(FACES):
        slab_send(s1.at[f], r1.at[f], send1.at[f], recv1.at[f])

    table_wait(5, 6, 7, 8, 9, 10, 11)
    zf0[...] = jnp.where(mixed_line, zf0[...].astype(F32), zf[...].astype(F32)).astype(BF)
    zi0[...] = jnp.where(mixed_line, zi0[...].astype(F32), zi[...].astype(F32)).astype(BF)

    def to_z(f, carry):
        wait_for(r1.at[f], recv1.at[f])
        parts = []
        for k in range(4):
            block = r1[f, :, k].reshape(256, 128)
            z = dot(zf[...], block)
            if k == 0:
                z = jnp.where(lane0, dot(zf0[...], block), z)
            parts.append(z.reshape(tiles, 8, 128))
        s2[f] = jnp.concatenate(parts, axis=1).astype(BF)
        tile_send(s2.at[f], r2.at[f], send2.at[f], recv2.at[f])
        return carry

    lax.fori_loop(0, FACES, to_z, 0)

    for f in range(FACES):
        wait_for(r2.at[f], recv2.at[f])
    row = lax.broadcasted_iota(jnp.int32, (8, 128), 0)
    lane = lax.broadcasted_iota(jnp.int32, (8, 128), 1)
    mixed_here = mixed_line & ((t == 0) | (t == tiles // 2))
    two_reals = (lane == 0) & (lax.rem(row, 4) == 0) & mixed_here
    real_row = row < 4

    for q in range(2):

        def correlate(i, carry):
            d = lax.rem(t + i, tiles)
            p = 2 * d + q
            a = r2[pairs_s[p, 1], pairs_s[p, 0]].astype(F32)
            b = r2[pairs_s[p, 3], pairs_s[p, 2]].astype(F32)
            parts = []
            for k in range(4):
                ak, bk = a[8 * k : 8 * k + 8], b[8 * k : 8 * k + 8]
                same = ak * bk
                turned = pltpu.roll(ak, 4, axis=0) * bk
                cross = jnp.where(
                    real_row,
                    same + pltpu.roll(same, 4, axis=0),
                    pltpu.roll(turned, 4, axis=0) - turned,
                )
                if k == 0:
                    cross = jnp.where(two_reals, same, cross)
                square = cross * cross
                total = square + pltpu.roll(square, 4, axis=0)
                if k == 0:
                    total = jnp.where(two_reals, square, total)
                parts.append(cross * lax.rsqrt(total + 1.0))
            s3[q, d] = jnp.concatenate(parts, axis=0).astype(BF)
            return carry

        lax.fori_loop(0, tiles, correlate, 0)
        tile_send(s3.at[q], r3.at[q], send3.at[q], recv3.at[q])

    def from_z(q, carry):
        wait_for(r3.at[q], recv3.at[q])
        got = r3[q].astype(F32)
        for k in range(4):
            block = got[:, 8 * k : 8 * k + 8].reshape(256, 128).astype(BF)
            w = dot(zi[...], block)
            if k == 0:
                w = jnp.where(lane0, dot(zi0[...], block), w)
            s4[q, :, k] = w.astype(BF).reshape(slabs, 32, 128)
        slab_send(s4.at[q], r4.at[q], send4.at[q], recv4.at[q])
        return carry

    lax.fori_loop(0, 2, from_z, 0)

    def from_x(q, carry):
        wait_for(r4.at[q], recv4.at[q])
        for half in range(2):
            block = r4[q, :, :, pl.ds(16 * half, 16), :].reshape(512, 128)
            v = dot(xi[...], block)
            v0 = dot(xi0[...], block)
            re = jnp.where(lane0, v0[:256], v[:256]).astype(BF)
            im = jnp.where(lane0, v0[256:], v[256:]).astype(BF)
            out[q, pl.ds(256 * half, 256), :] = dot(
                jnp.concatenate([re, im], axis=1), from_y[...]
            )
        return carry

    lax.fori_loop(0, 2, from_x, 0)

    for f in range(FACES):
        wait_for(s1.at[f, pl.ds(0, slabs - 1)], send1.at[f])
        wait_for(s2.at[f, pl.ds(0, tiles - 1)], send2.at[f])
    for q in range(2):
        wait_for(s3.at[q, pl.ds(0, tiles - 1)], send3.at[q])
        wait_for(s4.at[q, pl.ds(0, slabs - 1)], send4.at[q])


def solution(mesh):
    tiles, slabs = mesh.shape["tile"], mesh.shape["zslab"]

    def shards(band, pairs, extents):
        tables = constants()
        vmem = pl.BlockSpec(memory_space=pltpu.VMEM)
        smem = pl.BlockSpec(memory_space=pltpu.SMEM)
        anywhere = pl.BlockSpec(memory_space=pl.ANY)
        dma = pltpu.SemaphoreType.DMA
        scratch = [pltpu.VMEM((FACES, 1024, 512), BF)]
        scratch += [pltpu.VMEM(c.shape, BF) for c in tables]
        scratch += [pltpu.VMEM((FACES, slabs, 4, 32, 128), BF)] * 2
        scratch += [pltpu.VMEM((FACES, tiles, 32, 128), BF)] * 2
        scratch += [pltpu.VMEM((2, tiles, 32, 128), BF)] * 2
        scratch += [pltpu.VMEM((2, slabs, 4, 32, 128), BF)] * 2
        scratch += [dma((FACES,)), dma((12,))]
        scratch += [dma((FACES,))] * 4 + [dma((2,))] * 4
        maps = pl.pallas_call(
            functools.partial(body, tiles, slabs),
            out_shape=jax.ShapeDtypeStruct((2, 512, 256), F32),
            in_specs=[smem, vmem, vmem, anywhere] + [anywhere] * 12,
            out_specs=vmem,
            scratch_shapes=scratch,
            compiler_params=pltpu.CompilerParams(
                collective_id=0, has_side_effects=True, vmem_limit_bytes=48 << 20
            ),
        )(pairs, pairs, extents, band.reshape(FACES, 1024, 512), *tables)
        return maps.reshape(2, 16, GX, GY)

    placed = (P("tile", None, "zslab", None, None), P(), P())
    return jax.shard_map(
        shards,
        mesh=mesh,
        in_specs=placed,
        out_specs=P("tile", "zslab", None, None),
        check_vma=False,
    )
```

time: 221 us -> 88.3 us (0.40)
  waiting for transfers between devices: 116 us -> 0 us
  Pallas kernels: 0 us -> 74.2 us
  starting transfers between devices: 53.9 us -> 0 us
  matrix products: 19.9 us -> 0 us
  local copies, waits for them, and re-layouts: 26.5 us -> 13.7 us
  other arithmetic: 3.4 us -> 0 us
    all_to_all x8 -> x0, waiting for transfers between devices: 116 us -> none  [the longest x1 22.7 us: shards(): lax.all_to_all(out_im, 'tile', split_axis=0, concat_axis=0, tiled=True)]
    pallas_call x0 -> x1, Pallas kernels: none -> 74.2 us  [shards(): pl.pallas_call(functools.partial(body, tiles, slabs), out_shape=jax.Shape...]
    all_to_all x8 -> x0, starting transfers between devices: 53.9 us -> none  [the longest x1 10.5 us: shards(): lax.all_to_all(out_im, 'tile', split_axis=0, concat_axis=0, tiled=True)]
    dot_general x19 -> x0, matrix products: 19.9 us -> none  [product(): return jnp.einsum(form, left, right, preferred_element_type=jnp.float32)]
    unnamed x2 -> x27, local copies, waits for them, and re-layouts: 0.97 us -> 13.7 us
    convert_element_type x8 -> x0, local copies, waits for them, and re-layouts: 11.5 us -> none  [the longest x1 1.8 us: shards(): out_re = (product('szjk,zm->msjk', re_in, tables_z[0]) + product('szjk,zm...]
    reshape x1 -> x0, local copies, waits for them, and re-layouts: 7.21 us -> none  [shards(): image_volume = band.reshape(slots, zrows, 2 * GX, 2 * GY)]
    gather x4 -> x0, local copies, waits for them, and re-layouts: 4.39 us -> none  [the longest x1 1.1 us: cross_phase(): second_im = owner_im[second_tile_device, :, second_pos].astype(jnp.float32)]
  transfers between devices with their start and end apart: 8 -> 0, of which waited for: 8 -> 0; matrix products, arithmetic and copies ran while one was open for 5% -> 0% of each run, Pallas kernels for 0% -> 0%
where the time goes in v1:
time: 88.3 us; the launch traced here: 87.9 us
  Pallas kernels  74.2 us (84%)
  local copies, waits for them, and re-layouts  13.7 us (16%)
    pallas_call x1, Pallas kernels, shards(): pl.pallas_call(functools.partial(body, tiles, slabs), out_shape=jax.Shape...  74.2 us
    unnamed x27, local copies, waits for them, and re-layouts  13.7 us

profile of v1, /device:TPU:1, one launch (start us, length us, event | category | flops | bytes accessed | tf_op | source)
XLA Modules:
  0.0 87.9 jit_solution(14387200513808894984)
XLA Ops:
  0.0 0.8 copy.16.refs_0_.refs_1_
  0.8 0.8 copy.18.refs_2_
  1.5 0.0 copy-start
  1.5 1.0 %copy-done = bf16[512,512]{1,0:T(8,128)(2,1)S(1)} copy-done((bf16[512,512]{1,0:T(8,128)(2,1)S(1)}, bf16[512,512]{1,0:T(8,128)(2,1)}, u32[]{:S(2)}) %copy-start) | copy-done | bytes 524312
  2.6 0.0 copy-start.1
  2.6 1.0 %copy-done.1 = bf16[512,512]{1,0:T(8,128)(2,1)S(1)} copy-done((bf16[512,512]{1,0:T(8,128)(2,1)S(1)}, bf16[512,512]{1,0:T(8,128)(2,1)}, u32[]{:S(2)}) %copy-start.1) | copy-done | bytes 524312
  3.6 0.0 copy-start.2
  3.6 0.9 %copy-done.2 = bf16[512,256]{1,0:T(8,128)(2,1)S(1)} copy-done((bf16[512,256]{1,0:T(8,128)(2,1)S(1)}, bf16[512,256]{1,0:T(8,128)(2,1)}, u32[]{:S(2)}) %copy-start.2) | copy-done | bytes 262168
  4.6 0.0 copy-start.3
  4.6 0.9 %copy-done.3 = bf16[256,256]{1,0:T(8,128)(2,1)S(1)} copy-done((bf16[256,256]{1,0:T(8,128)(2,1)S(1)}, bf16[256,256]{1,0:T(8,128)(2,1)}, u32[]{:S(2)}) %copy-start.3) | copy-done | bytes 131096
  5.5 0.0 copy-start.4
  5.5 0.9 %copy-done.4 = bf16[256,256]{1,0:T(8,128)(2,1)S(1)} copy-done((bf16[256,256]{1,0:T(8,128)(2,1)S(1)}, bf16[256,256]{1,0:T(8,128)(2,1)}, u32[]{:S(2)}) %copy-start.4) | copy-done | bytes 131096
  6.4 0.0 copy-start.5
  6.4 0.9 %copy-done.5 = bf16[256,256]{1,0:T(8,128)(2,1)S(1)} copy-done((bf16[256,256]{1,0:T(8,128)(2,1)S(1)}, bf16[256,256]{1,0:T(8,128)(2,1)}, u32[]{:S(2)}) %copy-start.5) | copy-done | bytes 131096
  7.3 0.0 copy-start.6
  7.3 0.9 %copy-done.6 = bf16[256,256]{1,0:T(8,128)(2,1)S(1)} copy-done((bf16[256,256]{1,0:T(8,128)(2,1)S(1)}, bf16[256,256]{1,0:T(8,128)(2,1)}, u32[]{:S(2)}) %copy-start.6) | copy-done | bytes 131096
  8.2 0.0 copy-start.7
  8.2 0.9 %copy-done.7 = bf16[256,256]{1,0:T(8,128)(2,1)S(1)} copy-done((bf16[256,256]{1,0:T(8,128)(2,1)S(1)}, bf16[256,256]{1,0:T(8,128)(2,1)}, u32[]{:S(2)}) %copy-start.7) | copy-done | bytes 131096
  9.1 0.0 copy-start.8
  9.1 0.9 %copy-done.8 = bf16[256,256]{1,0:T(8,128)(2,1)S(1)} copy-done((bf16[256,256]{1,0:T(8,128)(2,1)S(1)}, bf16[256,256]{1,0:T(8,128)(2,1)}, u32[]{:S(2)}) %copy-start.8) | copy-done | bytes 131096
  10.0 0.0 copy-start.9
  10.0 0.9 %copy-done.9 = bf16[256,256]{1,0:T(8,128)(2,1)S(1)} copy-done((bf16[256,256]{1,0:T(8,128)(2,1)S(1)}, bf16[256,256]{1,0:T(8,128)(2,1)}, u32[]{:S(2)}) %copy-start.9) | copy-done | bytes 131096
  10.9 0.0 copy-start.10
  10.9 0.9 %copy-done.10 = bf16[256,256]{1,0:T(8,128)(2,1)S(1)} copy-done((bf16[256,256]{1,0:T(8,128)(2,1)S(1)}, bf16[256,256]{1,0:T(8,128)(2,1)}, u32[]{:S(2)}) %copy-start.10) | copy-done | bytes 131096
  11.8 0.0 copy-start.11
  11.8 0.9 %copy-done.11 = bf16[256,256]{1,0:T(8,128)(2,1)S(1)} copy-done((bf16[256,256]{1,0:T(8,128)(2,1)S(1)}, bf16[256,256]{1,0:T(8,128)(2,1)}, u32[]{:S(2)}) %copy-start.11) | copy-done | bytes 131096
  12.7 74.2 %shard_map.145 = f32[2,512,256]{2,1,0:T(8,128)S(1)} custom-call(s32[64,4]{1,0:T(8,128)S(1)} %copy.16.refs_0_.refs_1_, s32[64,4]{1,0:T(8,128)S(1)} %copy.16.refs_0_.refs_1_, s32[64,2]{1,0:T(8,128)S(1)} %copy.18.refs_2_, bf16[4,1024,512]{2,1,0:T(8,128)(2,1)} %bitcast.3, bf16[256,256]{1,0:T(8,128)(2,1)S(1)} %copy-done.11, bf16[512,256]{1,0:T(8,128)(2,1)S(1)} %copy-done.2, ...), custom_call_target="tpu_custom_call" | custom-call | tf_op jit(solution)/shard_map/pallas_call | solution.py:353
  87.0 1.0 %copy.20 = f32[2,16,32,256]{3,2,1,0:T(8,128)} copy(f32[2,16,32,256]{3,2,1,0:T(8,128)S(1)} %bitcast.2) | data formatting | bytes 2097152
Async XLA Ops:
  1.5 1.0 %copy-start = (bf16[512,512]{1,0:T(8,128)(2,1)S(1)}, bf16[512,512]{1,0:T(8,128)(2,1)}, u32[]{:S(2)}) copy-start(bf16[512,512]{1,0:T(8,128)(2,1)} %constant.34.clone.refs_14_) | copy-start | bytes 1572868
  2.6 1.0 %copy-start.1 = (bf16[512,512]{1,0:T(8,128)(2,1)S(1)}, bf16[512,512]{1,0:T(8,128)(2,1)}, u32[]{:S(2)}) copy-start(bf16[512,512]{1,0:T(8,128)(2,1)} %constant.33.clone.refs_13_) | copy-start | bytes 1572868
  3.6 0.9 %copy-start.2 = (bf16[512,256]{1,0:T(8,128)(2,1)S(1)}, bf16[512,256]{1,0:T(8,128)(2,1)}, u32[]{:S(2)}) copy-start(bf16[512,256]{1,0:T(8,128)(2,1)} %constant.25.clone.refs_5_) | copy-start | bytes 786436
  4.6 0.9 %copy-start.3 = (bf16[256,256]{1,0:T(8,128)(2,1)S(1)}, bf16[256,256]{1,0:T(8,128)(2,1)}, u32[]{:S(2)}) copy-start(bf16[256,256]{1,0:T(8,128)(2,1)} %constant.35.clone.refs_15_) | copy-start | bytes 393220
  5.5 0.9 %copy-start.4 = (bf16[256,256]{1,0:T(8,128)(2,1)S(1)}, bf16[256,256]{1,0:T(8,128)(2,1)}, u32[]{:S(2)}) copy-start(bf16[256,256]{1,0:T(8,128)(2,1)} %constant.32.clone.refs_12_) | copy-start | bytes 393220
  6.4 0.9 %copy-start.5 = (bf16[256,256]{1,0:T(8,128)(2,1)S(1)}, bf16[256,256]{1,0:T(8,128)(2,1)}, u32[]{:S(2)}) copy-start(bf16[256,256]{1,0:T(8,128)(2,1)} %constant.31.clone.refs_11_) | copy-start | bytes 393220
  7.3 0.9 %copy-start.6 = (bf16[256,256]{1,0:T(8,128)(2,1)S(1)}, bf16[256,256]{1,0:T(8,128)(2,1)}, u32[]{:S(2)}) copy-start(bf16[256,256]{1,0:T(8,128)(2,1)} %constant.30.clone.refs_10_) | copy-start | bytes 393220
  8.2 0.9 %copy-start.7 = (bf16[256,256]{1,0:T(8,128)(2,1)S(1)}, bf16[256,256]{1,0:T(8,128)(2,1)}, u32[]{:S(2)}) copy-start(bf16[256,256]{1,0:T(8,128)(2,1)} %constant.29.clone.refs_9_) | copy-start | bytes 393220
  9.1 0.9 %copy-start.8 = (bf16[256,256]{1,0:T(8,128)(2,1)S(1)}, bf16[256,256]{1,0:T(8,128)(2,1)}, u32[]{:S(2)}) copy-start(bf16[256,256]{1,0:T(8,128)(2,1)} %constant.28.clone.refs_8_) | copy-start | bytes 393220
  10.0 0.9 %copy-start.9 = (bf16[256,256]{1,0:T(8,128)(2,1)S(1)}, bf16[256,256]{1,0:T(8,128)(2,1)}, u32[]{:S(2)}) copy-start(bf16[256,256]{1,0:T(8,128)(2,1)} %constant.27.clone.refs_7_) | copy-start | bytes 393220
  10.9 0.9 %copy-start.10 = (bf16[256,256]{1,0:T(8,128)(2,1)S(1)}, bf16[256,256]{1,0:T(8,128)(2,1)}, u32[]{:S(2)}) copy-start(bf16[256,256]{1,0:T(8,128)(2,1)} %constant.26.clone.refs_6_) | copy-start | bytes 393220
  11.8 0.9 %copy-start.11 = (bf16[256,256]{1,0:T(8,128)(2,1)S(1)}, bf16[256,256]{1,0:T(8,128)(2,1)}, u32[]{:S(2)}) copy-start(bf16[256,256]{1,0:T(8,128)(2,1)} %constant.24.clone.refs_4_) | copy-start | bytes 393220

commit v2 on v1

--- a/solution.py
+++ b/solution.py
@@ -12,7 +12,11 @@
 
 GX, GY, GZ, FACES = 32, 256, 128, 4
 HALF = GY // 2
+VLIM = 52 << 20
 MESH = pl.DeviceIdType.MESH
+TABLE_ROWS = (256, 512, 256, 256, 256, 256, 256, 256, 256, 1024, 1024, 256)
+FIRST_ROWS = sum(TABLE_ROWS[:5])
+LATER_ROWS = sum(TABLE_ROWS[5:])
 BF = jnp.bfloat16
 F32 = jnp.float32
 
@@ -118,7 +122,8 @@
         x_inverse(doubled(x_line)),
         from_y,
     )
-    return tuple(t.astype(ml_dtypes.bfloat16) for t in tables)
+    tables = [t.reshape(-1, 256) if t.shape[1] == 256 else np.concatenate([t[:, :256], t[:, 256:]]) for t in tables]
+    return np.concatenate(tables).astype(ml_dtypes.bfloat16)
 
 
 def dot(a, b):
@@ -126,14 +131,14 @@
 
 
 def body(tiles, slabs, *refs):
-    (pairs_s, pairs_v, extents_v, band, *rest) = refs
-    hbm_tables, rest = rest[:12], rest[12:]
-    out, rest = rest[0], rest[1:]
-    raw, rest = rest[0], rest[1:]
-    tables, rest = rest[:12], rest[12:]
+    (pairs_s, pairs_hbm, extents_hbm, band, hbm_tables, out, raw, tables, pairs_v, extents_v, *rest) = refs
     s1, r1, s2, r2, s3, r3, s4, r4, raw_sem, table_sem, *sems = rest
     send1, recv1, send2, recv2, send3, recv3, send4, recv4 = sems
-    split, pool, to_y, xf, xf0, zf, zf0, zi, zi0, xi, xi0, from_y = tables
+    at, views = 0, []
+    for rows in TABLE_ROWS:
+        views.append(tables.at[pl.ds(at, rows)])
+        at += rows
+    split, pool, to_y, xf, xf0, zf, zf0, zi, zi0, xi, xi0, from_y = views
     t = lax.axis_index("tile")
     s = lax.axis_index("zslab")
 
@@ -151,14 +156,23 @@
             barrier, inc=1, device_id=(lax.rem(t + i, tiles), s), device_id_type=MESH
         )
 
+    fetches = [
+        pltpu.make_async_copy(
+            hbm_tables.at[pl.ds(0, FIRST_ROWS)], tables.at[pl.ds(0, FIRST_ROWS)], table_sem.at[0]
+        ),
+        pltpu.make_async_copy(pairs_hbm, pairs_v, table_sem.at[1]),
+        pltpu.make_async_copy(extents_hbm, extents_v, table_sem.at[2]),
+    ]
+    later = pltpu.make_async_copy(
+        hbm_tables.at[pl.ds(FIRST_ROWS, LATER_ROWS)],
+        tables.at[pl.ds(FIRST_ROWS, LATER_ROWS)],
+        table_sem.at[3],
+    )
+    for fetch in fetches:
+        fetch.start()
     for f in range(FACES):
         pltpu.make_async_copy(band.at[f], raw.at[f], raw_sem.at[f]).start()
-    for i in range(12):
-        pltpu.make_async_copy(hbm_tables[i], tables[i], table_sem.at[i]).start()
-
-    def table_wait(*which):
-        for i in which:
-            pltpu.make_async_copy(hbm_tables[i], tables[i], table_sem.at[i]).wait()
+    later.start()
 
     def slab_send(src, dst, send_sem, recv_sem):
         @pl.loop(1, slabs)
@@ -197,18 +211,19 @@
     two_lane0 = lax.broadcasted_iota(jnp.int32, (256, 256), 1) % 128 == 0
     mixed_line = (s == 0) | (s == slabs // 2)
 
-    first = pairs_v[:, 0:1] * FACES + pairs_v[:, 1:2]
-    second = pairs_v[:, 2:3] * FACES + pairs_v[:, 3:4]
+    for fetch in fetches:
+        fetch.wait()
+    first = pairs_v[0:1] * FACES + pairs_v[1:2]
+    second = pairs_v[2:3] * FACES + pairs_v[3:4]
     y_rows = lax.broadcasted_iota(jnp.int32, (512, 256), 0)
     x_lanes = lax.broadcasted_iota(jnp.int32, (256, 256), 1) % 64
 
-    table_wait(0, 1, 2, 3, 4)
-
-    def to_x(f, carry):
+
+    def to_x(f):
         slot = t * FACES + f
         named = (first == slot) | (second == slot)
-        ex = jnp.sum(jnp.where(named, extents_v[:, 0:1], 0), axis=0, keepdims=True)
-        ey = jnp.sum(jnp.where(named, extents_v[:, 1:2], 0), axis=0, keepdims=True)
+        ex = jnp.sum(jnp.where(named, extents_v[0:1], 0), axis=1, keepdims=True)
+        ey = jnp.sum(jnp.where(named, extents_v[1:2], 0), axis=1, keepdims=True)
         y_pool = jnp.where(y_rows < ey, pool[...].astype(F32), 0.0).astype(BF)
         x_split = jnp.where(x_lanes < ex, split[...].astype(F32), 0.0).astype(BF)
         pltpu.make_async_copy(band.at[f], raw.at[f], raw_sem.at[f]).wait()
@@ -231,20 +246,15 @@
             parts += [x[:, :128].reshape(32, 8, 128), x[:, 128:].reshape(32, 8, 128)]
         whole = jnp.concatenate(parts, axis=1).astype(BF)
         s1[f] = whole.reshape(slabs, 4, 32, 128)
-        return carry
-
-    lax.fori_loop(0, FACES, to_x, 0)
-
-    pl.semaphore_wait(barrier, slabs - 1 + tiles - 1)
-    for f in range(FACES):
-        slab_send(s1.at[f], r1.at[f], send1.at[f], recv1.at[f])
-
-    table_wait(5, 6, 7, 8, 9, 10, 11)
-    zf0[...] = jnp.where(mixed_line, zf0[...].astype(F32), zf[...].astype(F32)).astype(BF)
-    zi0[...] = jnp.where(mixed_line, zi0[...].astype(F32), zi[...].astype(F32)).astype(BF)
-
-    def to_z(f, carry):
+
+    def mix_tables():
+        later.wait()
+        zf0[...] = jnp.where(mixed_line, zf0[...].astype(F32), zf[...].astype(F32)).astype(BF)
+        zi0[...] = jnp.where(mixed_line, zi0[...].astype(F32), zi[...].astype(F32)).astype(BF)
+
+    def to_z(f):
         wait_for(r1.at[f], recv1.at[f])
+
         parts = []
         for k in range(4):
             block = r1[f, :, k].reshape(256, 128)
@@ -254,9 +264,29 @@
             parts.append(z.reshape(tiles, 8, 128))
         s2[f] = jnp.concatenate(parts, axis=1).astype(BF)
         tile_send(s2.at[f], r2.at[f], send2.at[f], recv2.at[f])
+
+    def forward(i, carry):
+        @pl.when(i < FACES)
+        def _():
+            to_x(i)
+
+            @pl.when(i == 0)
+            def _():
+                pl.semaphore_wait(barrier, slabs - 1 + tiles - 1)
+
+            slab_send(s1.at[i], r1.at[i], send1.at[i], recv1.at[i])
+
+            @pl.when(i == 0)
+            def _():
+                mix_tables()
+
+        @pl.when(i > 0)
+        def _():
+            to_z(i - 1)
+
         return carry
 
-    lax.fori_loop(0, FACES, to_z, 0)
+    lax.fori_loop(0, FACES + 1, forward, 0)
 
     for f in range(FACES):
         wait_for(r2.at[f], recv2.at[f])
@@ -271,8 +301,8 @@
         def correlate(i, carry):
             d = lax.rem(t + i, tiles)
             p = 2 * d + q
-            a = r2[pairs_s[p, 1], pairs_s[p, 0]].astype(F32)
-            b = r2[pairs_s[p, 3], pairs_s[p, 2]].astype(F32)
+            a = r2[pairs_s[1, p], pairs_s[0, p]].astype(F32)
+            b = r2[pairs_s[3, p], pairs_s[2, p]].astype(F32)
             parts = []
             for k in range(4):
                 ak, bk = a[8 * k : 8 * k + 8], b[8 * k : 8 * k + 8]
@@ -291,10 +321,22 @@
                     total = jnp.where(two_reals, square, total)
                 parts.append(cross * lax.rsqrt(total + 1.0))
             s3[q, d] = jnp.concatenate(parts, axis=0).astype(BF)
+
+            @pl.when(i < tiles)
+            def _():
+                pltpu.make_async_remote_copy(
+                    src_ref=s3.at[q, d],
+                    dst_ref=r3.at[q, t],
+                    send_sem=send3.at[q],
+                    recv_sem=recv3.at[q],
+                    device_id=(d, s),
+                    device_id_type=MESH,
+                ).start()
+
             return carry
 
-        lax.fori_loop(0, tiles, correlate, 0)
-        tile_send(s3.at[q], r3.at[q], send3.at[q], recv3.at[q])
+        lax.fori_loop(1, tiles + 1, correlate, 0)
+        pltpu.make_async_copy(s3.at[q, t], r3.at[q, t], recv3.at[q]).start()
 
     def from_z(q, carry):
         wait_for(r3.at[q], recv3.at[q])
@@ -314,8 +356,8 @@
         wait_for(r4.at[q], recv4.at[q])
         for half in range(2):
             block = r4[q, :, :, pl.ds(16 * half, 16), :].reshape(512, 128)
-            v = dot(xi[...], block)
-            v0 = dot(xi0[...], block)
+            v = dot(xi[:512], block[:256]) + dot(xi[512:], block[256:])
+            v0 = dot(xi0[:512], block[:256]) + dot(xi0[512:], block[256:])
             re = jnp.where(lane0, v0[:256], v[:256]).astype(BF)
             im = jnp.where(lane0, v0[256:], v[256:]).astype(BF)
             out[q, pl.ds(256 * half, 256), :] = dot(
@@ -343,23 +385,24 @@
         anywhere = pl.BlockSpec(memory_space=pl.ANY)
         dma = pltpu.SemaphoreType.DMA
         scratch = [pltpu.VMEM((FACES, 1024, 512), BF)]
-        scratch += [pltpu.VMEM(c.shape, BF) for c in tables]
+        scratch += [pltpu.VMEM(tables.shape, BF)]
+        scratch += [pltpu.VMEM((4, 64), jnp.int32), pltpu.VMEM((2, 64), jnp.int32)]
         scratch += [pltpu.VMEM((FACES, slabs, 4, 32, 128), BF)] * 2
         scratch += [pltpu.VMEM((FACES, tiles, 32, 128), BF)] * 2
         scratch += [pltpu.VMEM((2, tiles, 32, 128), BF)] * 2
         scratch += [pltpu.VMEM((2, slabs, 4, 32, 128), BF)] * 2
-        scratch += [dma((FACES,)), dma((12,))]
+        scratch += [dma((FACES,)), dma((4,))]
         scratch += [dma((FACES,))] * 4 + [dma((2,))] * 4
         maps = pl.pallas_call(
             functools.partial(body, tiles, slabs),
             out_shape=jax.ShapeDtypeStruct((2, 512, 256), F32),
-            in_specs=[smem, vmem, vmem, anywhere] + [anywhere] * 12,
+            in_specs=[smem] + [anywhere] * 4,
             out_specs=vmem,
             scratch_shapes=scratch,
             compiler_params=pltpu.CompilerParams(
-                collective_id=0, has_side_effects=True, vmem_limit_bytes=48 << 20
+                collective_id=0, has_side_effects=True, vmem_limit_bytes=VLIM
             ),
-        )(pairs, pairs, extents, band.reshape(FACES, 1024, 512), *tables)
+        )(pairs.T, pairs.T, extents.T, band.reshape(FACES, 1024, 512), tables)
         return maps.reshape(2, 16, GX, GY)
 
     placed = (P("tile", None, "zslab", None, None), P(), P())

time: 88.3 us -> 68.1 us (0.77)
  local copies, waits for them, and re-layouts: 13.7 us -> 2.33 us
  Pallas kernels: 74.2 us -> 65.7 us
    unnamed x27 -> x5, local copies, waits for them, and re-layouts: 13.7 us -> 2.33 us
    pallas_call x1, Pallas kernels: 74.2 us -> 65.7 us  [shards(): pl.pallas_call(functools.partial(body, tiles, slabs), out_shape=jax.Shape...]
where the time goes in v2:
time: 68.1 us; the launch traced here: 68 us
  Pallas kernels  65.7 us (96%)
  local copies, waits for them, and re-layouts  2.33 us (3%)
    pallas_call x1, Pallas kernels, shards(): pl.pallas_call(functools.partial(body, tiles, slabs), out_shape=jax.Shape...  65.7 us
    unnamed x5, local copies, waits for them, and re-layouts  2.33 us

profile of v2, /device:TPU:1, one launch (start us, length us, event | category | flops | bytes accessed | tf_op | source)
XLA Modules:
  0.0 68.0 jit_solution(168749607733034346)
XLA Ops:
  0.0 0.0 copy-start
  0.0 0.7 copy-done
  0.7 0.0 copy-start.1
  0.7 0.7 copy-done.1
  1.4 65.7 %shard_map.46 = f32[2,512,256]{2,1,0:T(8,128)S(1)} custom-call(s32[4,64]{1,0:T(4,128)S(1)} %bitcast.5, s32[4,64]{1,0:T(4,128)S(1)} %bitcast.6, s32[2,64]{1,0:T(2,128)S(1)} %bitcast.7, bf16[4,1024,512]{2,1,0:T(8,128)(2,1)} %bitcast.8, bf16[4864,256]{1,0:T(8,128)(2,1)} %constant.2.clone.refs_4_), custom_call_target="tpu_custom_call" | custom-call | tf_op jit(solution)/shard_map/pallas_call | solution.py:396
  67.0 1.0 %copy.6 = f32[2,16,32,256]{3,2,1,0:T(8,128)} copy(f32[2,16,32,256]{3,2,1,0:T(8,128)S(1)} %bitcast.4) | data formatting | bytes 2097152
Async XLA Ops:
  0.0 0.7 %copy-start = (s32[64,4]{0,1:T(4,128)S(1)}, s32[64,4]{0,1:T(4,128)}, u32[]{:S(2)}) copy-start(s32[64,4]{0,1:T(4,128)} %param.5) | copy-start | bytes 3076
  0.7 0.7 copy-start.1

commit v3 on v2

--- a/solution.py
+++ b/solution.py
@@ -102,7 +102,8 @@
 
     def x_inverse(m):
         e = eye8.reshape(8, 2, 4)
-        return np.einsum("xpkq,zgw->pzxkgqw", m, e).reshape(512, 512)
+        m = np.einsum("xpkq,zgw->pzxkgqw", m, e).reshape(512, 8, 2, 32)
+        return np.transpose(m, (0, 2, 1, 3)).reshape(512, 512)
 
     from_y = np.concatenate([2.0 * cy[:HALF], -2.0 * sy[:HALF]], axis=0)
     from_y[0], from_y[HALF] = cy[0], cy[HALF]
@@ -131,13 +132,14 @@
 
 
 def body(tiles, slabs, *refs):
-    (pairs_s, pairs_hbm, extents_hbm, band, hbm_tables, out, raw, tables, pairs_v, extents_v, *rest) = refs
-    s1, r1, s2, r2, s3, r3, s4, r4, raw_sem, table_sem, *sems = rest
+    (pairs_hbm, extents_hbm, band, hbm_tables, out, raw, tables, pairs_v, extents_v, *rest) = refs
+    s1, r1, s2, r2_first, r2_second, s3, r3, s4, r4, pairs_s, raw_sem, table_sem, *sems = rest
     send1, recv1, send2, recv2, send3, recv3, send4, recv4 = sems
     at, views = 0, []
     for rows in TABLE_ROWS:
         views.append(tables.at[pl.ds(at, rows)])
         at += rows
+    r2 = (r2_first, r2_second)
     split, pool, to_y, xf, xf0, zf, zf0, zi, zi0, xi, xi0, from_y = views
     t = lax.axis_index("tile")
     s = lax.axis_index("zslab")
@@ -173,6 +175,8 @@
     for f in range(FACES):
         pltpu.make_async_copy(band.at[f], raw.at[f], raw_sem.at[f]).start()
     later.start()
+    index = pltpu.make_async_copy(pairs_hbm, pairs_s, table_sem.at[4])
+    index.start()
 
     def slab_send(src, dst, send_sem, recv_sem):
         @pl.loop(1, slabs)
@@ -245,25 +249,29 @@
             x = jnp.where(two_lane0, dot(xf0[...], stacked), dot(xf[...], stacked))
             parts += [x[:, :128].reshape(32, 8, 128), x[:, 128:].reshape(32, 8, 128)]
         whole = jnp.concatenate(parts, axis=1).astype(BF)
-        s1[f] = whole.reshape(slabs, 4, 32, 128)
+        whole = whole.reshape(slabs, 2, 2, 32, 128)
+        for h in range(2):
+            s1[h, f] = whole[:, h]
 
     def mix_tables():
         later.wait()
+        index.wait()
         zf0[...] = jnp.where(mixed_line, zf0[...].astype(F32), zf[...].astype(F32)).astype(BF)
         zi0[...] = jnp.where(mixed_line, zi0[...].astype(F32), zi[...].astype(F32)).astype(BF)
 
-    def to_z(f):
-        wait_for(r1.at[f], recv1.at[f])
-
-        parts = []
-        for k in range(4):
-            block = r1[f, :, k].reshape(256, 128)
-            z = dot(zf[...], block)
-            if k == 0:
-                z = jnp.where(lane0, dot(zf0[...], block), z)
-            parts.append(z.reshape(tiles, 8, 128))
-        s2[f] = jnp.concatenate(parts, axis=1).astype(BF)
-        tile_send(s2.at[f], r2.at[f], send2.at[f], recv2.at[f])
+    def to_z(h, f):
+        wait_for(r1.at[h, f], recv1.at[h, f])
+        blocks = [r1[h, f, :, k].reshape(256, 128) for k in range(2)]
+        z = dot(zf[...], jnp.concatenate(blocks, axis=1))
+        parts = [z[:, :128], z[:, 128:]]
+        if h == 0:
+            parts[0] = jnp.where(lane0, dot(zf0[...], blocks[0]), parts[0])
+        parts = [p.reshape(tiles, 8, 128) for p in parts]
+        s2[h, f] = jnp.concatenate(parts, axis=1).astype(BF)
+        tile_send(s2.at[h, f], r2[h].at[f], send2.at[h, f], recv2.at[h, f])
+
+    def send_slot(h, f):
+        slab_send(s1.at[h, f], r1.at[h, f], send1.at[h, f], recv1.at[h, f])
 
     def forward(i, carry):
         @pl.when(i < FACES)
@@ -274,7 +282,7 @@
             def _():
                 pl.semaphore_wait(barrier, slabs - 1 + tiles - 1)
 
-            slab_send(s1.at[i], r1.at[i], send1.at[i], recv1.at[i])
+            send_slot(0, i)
 
             @pl.when(i == 0)
             def _():
@@ -282,29 +290,37 @@
 
         @pl.when(i > 0)
         def _():
-            to_z(i - 1)
+            to_z(0, i - 1)
+            send_slot(1, i - 1)
 
         return carry
 
     lax.fori_loop(0, FACES + 1, forward, 0)
 
-    for f in range(FACES):
-        wait_for(r2.at[f], recv2.at[f])
+    def forward_rest(f, carry):
+        to_z(1, f)
+        return carry
+
+    lax.fori_loop(0, FACES, forward_rest, 0)
+
     row = lax.broadcasted_iota(jnp.int32, (8, 128), 0)
     lane = lax.broadcasted_iota(jnp.int32, (8, 128), 1)
     mixed_here = mixed_line & ((t == 0) | (t == tiles // 2))
     two_reals = (lane == 0) & (lax.rem(row, 4) == 0) & mixed_here
     real_row = row < 4
 
-    for q in range(2):
+    def cross_half(h):
+        for f in range(FACES):
+            wait_for(r2[h].at[f], recv2.at[h, f])
 
         def correlate(i, carry):
-            d = lax.rem(t + i, tiles)
+            q = lax.div(i, tiles)
+            d = lax.rem(t + 1 + i, tiles)
             p = 2 * d + q
-            a = r2[pairs_s[1, p], pairs_s[0, p]].astype(F32)
-            b = r2[pairs_s[3, p], pairs_s[2, p]].astype(F32)
+            a = r2[h][pairs_s[1, p], pairs_s[0, p]].astype(F32)
+            b = r2[h][pairs_s[3, p], pairs_s[2, p]].astype(F32)
             parts = []
-            for k in range(4):
+            for k in range(2):
                 ak, bk = a[8 * k : 8 * k + 8], b[8 * k : 8 * k + 8]
                 same = ak * bk
                 turned = pltpu.roll(ak, 4, axis=0) * bk
@@ -313,51 +329,61 @@
                     same + pltpu.roll(same, 4, axis=0),
                     pltpu.roll(turned, 4, axis=0) - turned,
                 )
-                if k == 0:
+                mixed = h == 0 and k == 0
+                if mixed:
                     cross = jnp.where(two_reals, same, cross)
                 square = cross * cross
                 total = square + pltpu.roll(square, 4, axis=0)
-                if k == 0:
+                if mixed:
                     total = jnp.where(two_reals, square, total)
                 parts.append(cross * lax.rsqrt(total + 1.0))
-            s3[q, d] = jnp.concatenate(parts, axis=0).astype(BF)
-
-            @pl.when(i < tiles)
+            s3[h, q, d] = jnp.concatenate(parts, axis=0).astype(BF)
+
+            @pl.when(lax.rem(i, tiles) < tiles - 1)
             def _():
                 pltpu.make_async_remote_copy(
-                    src_ref=s3.at[q, d],
-                    dst_ref=r3.at[q, t],
-                    send_sem=send3.at[q],
-                    recv_sem=recv3.at[q],
+                    src_ref=s3.at[h, q, d],
+                    dst_ref=r3.at[h, q, t],
+                    send_sem=send3.at[h, q],
+                    recv_sem=recv3.at[h, q],
                     device_id=(d, s),
                     device_id_type=MESH,
                 ).start()
 
             return carry
 
-        lax.fori_loop(1, tiles + 1, correlate, 0)
-        pltpu.make_async_copy(s3.at[q, t], r3.at[q, t], recv3.at[q]).start()
-
-    def from_z(q, carry):
-        wait_for(r3.at[q], recv3.at[q])
-        got = r3[q].astype(F32)
-        for k in range(4):
-            block = got[:, 8 * k : 8 * k + 8].reshape(256, 128).astype(BF)
-            w = dot(zi[...], block)
-            if k == 0:
-                w = jnp.where(lane0, dot(zi0[...], block), w)
-            s4[q, :, k] = w.astype(BF).reshape(slabs, 32, 128)
-        slab_send(s4.at[q], r4.at[q], send4.at[q], recv4.at[q])
-        return carry
-
-    lax.fori_loop(0, 2, from_z, 0)
+        lax.fori_loop(0, 2 * tiles, correlate, 0)
+        for q in range(2):
+            pltpu.make_async_copy(s3.at[h, q, t], r3.at[h, q, t], recv3.at[h, q]).start()
+
+    cross_half(0)
+    cross_half(1)
+
+    def from_z(h, q):
+        wait_for(r3.at[h, q], recv3.at[h, q])
+        got = r3[h, q].astype(F32)
+        blocks = [got[:, 8 * k : 8 * k + 8].reshape(256, 128).astype(BF) for k in range(2)]
+        w = dot(zi[...], jnp.concatenate(blocks, axis=1))
+        parts = [w[:, :128], w[:, 128:]]
+        if h == 0:
+            parts[0] = jnp.where(lane0, dot(zi0[...], blocks[0]), parts[0])
+        for k in range(2):
+            s4[h, q, :, k] = parts[k].astype(BF).reshape(slabs, 32, 128)
+        slab_send(s4.at[h, q], r4.at[h, q], send4.at[h, q], recv4.at[h, q])
+
+    for h in range(2):
+        for q in range(2):
+            from_z(h, q)
 
     def from_x(q, carry):
-        wait_for(r4.at[q], recv4.at[q])
+        for h in range(2):
+            wait_for(r4.at[h, q], recv4.at[h, q])
         for half in range(2):
-            block = r4[q, :, :, pl.ds(16 * half, 16), :].reshape(512, 128)
-            v = dot(xi[:512], block[:256]) + dot(xi[512:], block[256:])
-            v0 = dot(xi0[:512], block[:256]) + dot(xi0[512:], block[256:])
+            blocks = [
+                r4[h, q, :, :, pl.ds(16 * half, 16), :].reshape(256, 128) for h in range(2)
+            ]
+            v = dot(xi[:512], blocks[0]) + dot(xi[512:], blocks[1])
+            v0 = dot(xi0[:512], blocks[0]) + dot(xi0[512:], blocks[1])
             re = jnp.where(lane0, v0[:256], v[:256]).astype(BF)
             im = jnp.where(lane0, v0[256:], v[256:]).astype(BF)
             out[q, pl.ds(256 * half, 256), :] = dot(
@@ -367,12 +393,13 @@
 
     lax.fori_loop(0, 2, from_x, 0)
 
-    for f in range(FACES):
-        wait_for(s1.at[f, pl.ds(0, slabs - 1)], send1.at[f])
-        wait_for(s2.at[f, pl.ds(0, tiles - 1)], send2.at[f])
-    for q in range(2):
-        wait_for(s3.at[q, pl.ds(0, tiles - 1)], send3.at[q])
-        wait_for(s4.at[q, pl.ds(0, slabs - 1)], send4.at[q])
+    for h in range(2):
+        for f in range(FACES):
+            wait_for(s1.at[h, f, pl.ds(0, slabs - 1)], send1.at[h, f])
+            wait_for(s2.at[h, f, pl.ds(0, tiles - 1)], send2.at[h, f])
+        for q in range(2):
+            wait_for(s3.at[h, q, pl.ds(0, tiles - 1)], send3.at[h, q])
+            wait_for(s4.at[h, q, pl.ds(0, slabs - 1)], send4.at[h, q])
 
 
 def solution(mesh):
@@ -381,28 +408,28 @@
     def shards(band, pairs, extents):
         tables = constants()
         vmem = pl.BlockSpec(memory_space=pltpu.VMEM)
-        smem = pl.BlockSpec(memory_space=pltpu.SMEM)
-        anywhere = pl.BlockSpec(memory_space=pl.ANY)
+        hbm = pl.BlockSpec(memory_space=pltpu.HBM)
         dma = pltpu.SemaphoreType.DMA
         scratch = [pltpu.VMEM((FACES, 1024, 512), BF)]
         scratch += [pltpu.VMEM(tables.shape, BF)]
         scratch += [pltpu.VMEM((4, 64), jnp.int32), pltpu.VMEM((2, 64), jnp.int32)]
-        scratch += [pltpu.VMEM((FACES, slabs, 4, 32, 128), BF)] * 2
-        scratch += [pltpu.VMEM((FACES, tiles, 32, 128), BF)] * 2
-        scratch += [pltpu.VMEM((2, tiles, 32, 128), BF)] * 2
-        scratch += [pltpu.VMEM((2, slabs, 4, 32, 128), BF)] * 2
-        scratch += [dma((FACES,)), dma((4,))]
-        scratch += [dma((FACES,))] * 4 + [dma((2,))] * 4
+        scratch += [pltpu.VMEM((2, FACES, slabs, 2, 32, 128), BF)] * 2
+        scratch += [pltpu.VMEM((2, FACES, tiles, 16, 128), BF)]
+        scratch += [pltpu.VMEM((FACES, tiles, 16, 128), BF)] * 2
+        scratch += [pltpu.VMEM((2, 2, tiles, 16, 128), BF)] * 2
+        scratch += [pltpu.VMEM((2, 2, slabs, 2, 32, 128), BF)] * 2
+        scratch += [pltpu.SMEM((4, 64), jnp.int32), dma((FACES,)), dma((5,))]
+        scratch += [dma((2, FACES))] * 4 + [dma((2, 2))] * 4
         maps = pl.pallas_call(
             functools.partial(body, tiles, slabs),
             out_shape=jax.ShapeDtypeStruct((2, 512, 256), F32),
-            in_specs=[smem] + [anywhere] * 4,
+            in_specs=[hbm] * 4,
             out_specs=vmem,
             scratch_shapes=scratch,
             compiler_params=pltpu.CompilerParams(
                 collective_id=0, has_side_effects=True, vmem_limit_bytes=VLIM
             ),
-        )(pairs.T, pairs.T, extents.T, band.reshape(FACES, 1024, 512), tables)
+        )(pltpu.with_memory_space_constraint(pairs.T, pltpu.HBM), pltpu.with_memory_space_constraint(extents.T, pltpu.HBM), band.reshape(FACES, 1024, 512), tables)
         return maps.reshape(2, 16, GX, GY)
 
     placed = (P("tile", None, "zslab", None, None), P(), P())

time: 68.1 us -> 63 us (0.925)
  Pallas kernels: 65.7 us -> 62 us
  local copies, waits for them, and re-layouts: 2.33 us -> 0.97 us
    pallas_call x1, Pallas kernels: 65.7 us -> 62 us  [shards(): pl.pallas_call(functools.partial(body, tiles, slabs), out_shape=jax.Shape...]
    unnamed x5 -> x1, local copies, waits for them, and re-layouts: 2.33 us -> 0.97 us
where the time goes in v3:
time: 63 us; the launch traced here: 62.9 us
  Pallas kernels  62 us (98%)
  local copies, waits for them, and re-layouts  0.97 us (2%)
    pallas_call x1, Pallas kernels, shards(): pl.pallas_call(functools.partial(body, tiles, slabs), out_shape=jax.Shape...  62 us

profile of v3, /device:TPU:1, one launch (start us, length us, event | category | flops | bytes accessed | tf_op | source)
XLA Modules:
  0.0 62.9 jit_solution(8686294205495650869)
XLA Ops:
  0.0 62.0 %shard_map.46 = f32[2,512,256]{2,1,0:T(8,128)S(1)} custom-call(s32[4,64]{1,0:T(4,128)} %bitcast.6, s32[2,64]{1,0:T(2,128)} %bitcast.7, bf16[4,1024,512]{2,1,0:T(8,128)(2,1)} %bitcast.5, bf16[4864,256]{1,0:T(8,128)(2,1)} %constant.2.clone.refs_3_), custom_call_target="tpu_custom_call" | custom-call | tf_op jit(solution)/shard_map/pallas_call | solution.py:423
  62.0 1.0 %copy.6 = f32[2,16,32,256]{3,2,1,0:T(8,128)} copy(f32[2,16,32,256]{3,2,1,0:T(8,128)S(1)} %bitcast.4) | data formatting | bytes 2097152

commit v4 on v3

--- a/solution.py
+++ b/solution.py
@@ -14,9 +14,9 @@
 HALF = GY // 2
 VLIM = 52 << 20
 MESH = pl.DeviceIdType.MESH
-TABLE_ROWS = (256, 512, 256, 256, 256, 256, 256, 256, 256, 1024, 1024, 256)
-FIRST_ROWS = sum(TABLE_ROWS[:5])
-LATER_ROWS = sum(TABLE_ROWS[5:])
+TABLE_ROWS = (512, 256, 256, 256, 256, 256, 256, 256, 1024, 1024, 256)
+FIRST_ROWS = sum(TABLE_ROWS[:4])
+LATER_ROWS = sum(TABLE_ROWS[4:])
 BF = jnp.bfloat16
 F32 = jnp.float32
 
@@ -85,10 +85,6 @@
     pool = np.repeat(0.5 * np.eye(GY, dtype=np.float32), 2, axis=0)
     eye4, eye8 = np.eye(4, dtype=np.float32), np.eye(8, dtype=np.float32)
 
-    split = np.zeros((2, 4, GX, 4, GX, 2), np.float32)
-    for parity in (0, 1):
-        split[parity, ..., parity] = np.einsum("zw,xv->zxwv", eye4, np.eye(GX, dtype=np.float32))
-
     def x_forward(m):
         return np.einsum("kpxq,zw->kpzqwx", m, eye4).reshape(256, 256)
 
@@ -110,7 +106,6 @@
     z_line = line_pair_forward(cz, sz)
     x_line = real_pair_forward(cx, sx)
     tables = (
-        split.reshape(256, 256),
         pool,
         to_y,
         x_forward(complex_forward(cx, sx)),
@@ -133,14 +128,14 @@
 
 def body(tiles, slabs, *refs):
     (pairs_hbm, extents_hbm, band, hbm_tables, out, raw, tables, pairs_v, extents_v, *rest) = refs
-    s1, r1, s2, r2_first, r2_second, s3, r3, s4, r4, pairs_s, raw_sem, table_sem, *sems = rest
+    s1, r1, s2, r2_first, r2_second, s3, r3, s4, r4, pairs_s, halved, partial, raw_sem, table_sem, *sems = rest
     send1, recv1, send2, recv2, send3, recv3, send4, recv4 = sems
     at, views = 0, []
     for rows in TABLE_ROWS:
         views.append(tables.at[pl.ds(at, rows)])
         at += rows
     r2 = (r2_first, r2_second)
-    split, pool, to_y, xf, xf0, zf, zf0, zi, zi0, xi, xi0, from_y = views
+    pool, to_y, xf, xf0, zf, zf0, zi, zi0, xi, xi0, from_y = views
     t = lax.axis_index("tile")
     s = lax.axis_index("zslab")
 
@@ -213,6 +208,7 @@
 
     lane0 = lax.broadcasted_iota(jnp.int32, (256, 128), 1) == 0
     two_lane0 = lax.broadcasted_iota(jnp.int32, (256, 256), 1) % 128 == 0
+    wide_lane0 = lax.broadcasted_iota(jnp.int32, (512, 128), 1) == 0
     mixed_line = (s == 0) | (s == slabs // 2)
 
     for fetch in fetches:
@@ -220,7 +216,7 @@
     first = pairs_v[0:1] * FACES + pairs_v[1:2]
     second = pairs_v[2:3] * FACES + pairs_v[3:4]
     y_rows = lax.broadcasted_iota(jnp.int32, (512, 256), 0)
-    x_lanes = lax.broadcasted_iota(jnp.int32, (256, 256), 1) % 64
+    x_even = lax.broadcasted_iota(jnp.int32, (128, 256), 0) % 32 * 2
 
 
     def to_x(f):
@@ -229,15 +225,22 @@
         ex = jnp.sum(jnp.where(named, extents_v[0:1], 0), axis=1, keepdims=True)
         ey = jnp.sum(jnp.where(named, extents_v[1:2], 0), axis=1, keepdims=True)
         y_pool = jnp.where(y_rows < ey, pool[...].astype(F32), 0.0).astype(BF)
-        x_split = jnp.where(x_lanes < ex, split[...].astype(F32), 0.0).astype(BF)
+        even_live, odd_live = x_even < ex, x_even + 1 < ex
         pltpu.make_async_copy(band.at[f], raw.at[f], raw_sem.at[f]).wait()
         parts = []
         for half in range(2):
             y = []
             for g in range(2):
                 rows = raw[f, pl.ds(512 * half + 256 * g, 256), :]
-                parted = dot(x_split, rows).astype(BF)
-                down = (dot(parted[:128], y_pool) + dot(parted[128:], y_pool)).astype(BF)
+                summed = dot(rows, y_pool)
+                even, odd = [], []
+                for w in range(2):
+                    halved[half, g, w] = summed[:, 128 * w : 128 * w + 128]
+                    even.append(halved[half, g, w, pl.ds(0, 128, stride=2), :])
+                    odd.append(halved[half, g, w, pl.ds(1, 128, stride=2), :])
+                even = jnp.where(even_live, jnp.concatenate(even, axis=1), 0.0)
+                odd = jnp.where(odd_live, jnp.concatenate(odd, axis=1), 0.0)
+                down = (even + odd).astype(BF)
                 y.append(dot(down, to_y[...]).astype(BF))
             stacked = jnp.concatenate(
                 [
@@ -371,27 +374,25 @@
             s4[h, q, :, k] = parts[k].astype(BF).reshape(slabs, 32, 128)
         slab_send(s4.at[h, q], r4.at[h, q], send4.at[h, q], recv4.at[h, q])
 
+    def from_x(h, q):
+        wait_for(r4.at[h, q], recv4.at[h, q])
+        for half in range(2):
+            block = r4[h, q, :, :, pl.ds(16 * half, 16), :].reshape(256, 128)
+            rows = pl.ds(512 * h, 512)
+            v = jnp.where(wide_lane0, dot(xi0[rows], block), dot(xi[rows], block))
+            if h == 0:
+                partial[q, half] = v
+                continue
+            v = (partial[q, half] + v).astype(BF)
+            out[q, pl.ds(256 * half, 256), :] = dot(
+                jnp.concatenate([v[:256], v[256:]], axis=1), from_y[...]
+            )
+
     for h in range(2):
         for q in range(2):
             from_z(h, q)
-
-    def from_x(q, carry):
-        for h in range(2):
-            wait_for(r4.at[h, q], recv4.at[h, q])
-        for half in range(2):
-            blocks = [
-                r4[h, q, :, :, pl.ds(16 * half, 16), :].reshape(256, 128) for h in range(2)
-            ]
-            v = dot(xi[:512], blocks[0]) + dot(xi[512:], blocks[1])
-            v0 = dot(xi0[:512], blocks[0]) + dot(xi0[512:], blocks[1])
-            re = jnp.where(lane0, v0[:256], v[:256]).astype(BF)
-            im = jnp.where(lane0, v0[256:], v[256:]).astype(BF)
-            out[q, pl.ds(256 * half, 256), :] = dot(
-                jnp.concatenate([re, im], axis=1), from_y[...]
-            )
-        return carry
-
-    lax.fori_loop(0, 2, from_x, 0)
+        for q in range(2):
+            from_x(h, q)
 
     for h in range(2):
         for f in range(FACES):
@@ -418,7 +419,7 @@
         scratch += [pltpu.VMEM((FACES, tiles, 16, 128), BF)] * 2
         scratch += [pltpu.VMEM((2, 2, tiles, 16, 128), BF)] * 2
         scratch += [pltpu.VMEM((2, 2, slabs, 2, 32, 128), BF)] * 2
-        scratch += [pltpu.SMEM((4, 64), jnp.int32), dma((FACES,)), dma((5,))]
+        scratch += [pltpu.SMEM((4, 64), jnp.int32), pltpu.VMEM((2, 2, 2, 256, 128), F32), pltpu.VMEM((2, 2, 512, 128), F32), dma((FACES,)), dma((5,))]
         scratch += [dma((2, FACES))] * 4 + [dma((2, 2))] * 4
         maps = pl.pallas_call(
             functools.partial(body, tiles, slabs),

time: 63 us -> 62 us (0.984)
  Pallas kernels: 62 us -> 61 us
    pallas_call x1, Pallas kernels: 62 us -> 61 us  [shards(): pl.pallas_call(functools.partial(body, tiles, slabs), out_shape=jax.Shape...]
where the time goes in v4:
time: 62 us
  Pallas kernels  61 us (98%)
  local copies, waits for them, and re-layouts  0.97 us (2%)
    pallas_call x1, Pallas kernels, shards(): pl.pallas_call(functools.partial(body, tiles, slabs), out_shape=jax.Shape...  61 us

profile of v4, /device:TPU:1, one launch (start us, length us, event | category | flops | bytes accessed | tf_op | source)
XLA Modules:
  0.0 62.0 jit_solution(8639615035296041496)
XLA Ops:
  0.0 61.0 %shard_map.46 = f32[2,512,256]{2,1,0:T(8,128)S(1)} custom-call(s32[4,64]{1,0:T(4,128)} %bitcast.6, s32[2,64]{1,0:T(2,128)} %bitcast.7, bf16[4,1024,512]{2,1,0:T(8,128)(2,1)} %bitcast.5, bf16[4608,256]{1,0:T(8,128)(2,1)} %constant.2.clone.refs_3_), custom_call_target="tpu_custom_call" | custom-call | tf_op jit(solution)/shard_map/pallas_call | solution.py:424
  61.0 1.0 %copy.6 = f32[2,16,32,256]{3,2,1,0:T(8,128)} copy(f32[2,16,32,256]{3,2,1,0:T(8,128)S(1)} %bitcast.4) | data formatting | bytes 2097152
